TPU v7x, 32 devices: a whole 2x2x4 slice. The times are simulated.
32 devices in a mesh: groups: 2 (over y), wide: 16 (over z, x, core).
Axes of the slice: x: 2, y: 2, z: 4, core: 2. Of those that a mesh axis runs over, the one named last changes fastest.
Arguments:
- bfac: bfloat16 [32, 256, 4, 4096], P('wide', None, 'groups'), parts along dimension 2, may hold values from -2 to 2
- pair_mask: int32 [32, 3], P('wide'), may hold values 0 or 1
- dom_start: int32 [32, 3], P('wide'), may hold values from 0 to 16
Outputs:
- kband: float32 [64, 3, 256, 256], P(('groups', 'wide')), parts along dimension 0
- kmirror: float32 [64, 2, 256, 256], P(('groups', 'wide')), parts along dimension 0
There are 2 independent parts, one for each index of `groups`. A program takes and returns all parts, laid end to end along the dimension named above; an argument that names none is the same for every part. Nothing has to cross between parts.
All inputs are finite; a program needn't handle non-finite values. No bound on the sum of `pair_mask` on one device may be relied on, other than what follows from the above.
Results may differ from a plain program's by a relative error of at most 0.0003.
Values may be sent and summed in bfloat16 or wider, within the bound.
No kernel may reach another device: no remote copies, remote signals or barrier semaphores. Data moves between devices by JAX's collectives and lax.ppermute only.
A program may use at most 128 MiB of HBM per device.

v0:
```python
import functools

import jax
import jax.numpy as jnp
from jax import lax
from jax.experimental import pallas as pl
from jax.experimental.pallas import tpu as pltpu
from jax.sharding import PartitionSpec as P

DOM = 2048
DSTEP = 128
UNITS = DOM // DSTEP
SPARE = UNITS // 2
LEVELS = (0, 1, 2, 3, 4, 6, 8)
PER = 12
VMEM = pl.BlockSpec(memory_space=pltpu.VMEM)
SMEM = pl.BlockSpec(memory_space=pltpu.SMEM)
HBM = pl.BlockSpec(memory_space=pltpu.HBM)


def flags(screen, device, block, r):
    at = block * 3 + r
    return screen[device, at], screen[device, at + PER // 2]


def boundary(screen, device):
    m1, s1 = flags(screen, device, 0, 2)
    m2, s2 = flags(screen, device, 1, 1)
    m3, s3 = flags(screen, device, 1, 2)
    w1 = jnp.where(m1 > 0, s1, s2)
    w3 = jnp.where(m3 > 0, s3, s2)
    low, high = s2, s2 + UNITS
    for w in (w1, w3):
        low, high = (
            jnp.where(w <= s2, jnp.maximum(low, w + UNITS), low),
            jnp.where(w > s2, jnp.minimum(high, w), high),
        )
    rest = jnp.maximum(high - low, 0) * m2
    half = lax.shift_right_logical(rest + 1, 1)
    return dict(m1=m1, s1=s1, m2=m2, s2=s2, m3=m3, s3=s3, w1=w1, w3=w3, low=low, half=half, rest=rest)


def slow_plan(screen, n):
    me = lax.axis_index("wide")
    odd = lax.rem(me, 2)
    is_odd = odd == 1
    lower = jnp.where(is_odd, me, jnp.maximum(me - 1, 0))
    exists = jnp.where(is_odd, me < n - 1, me > 0).astype(jnp.int32)
    b = boundary(screen, lower)
    pick = lambda a, c: jnp.where(is_odd, a, c)
    mid = b["low"] + b["half"]
    other = b["rest"] - b["half"]
    recv_at = pick(b["w1"], b["w3"])
    first = jnp.maximum(b["s2"], recv_at)
    last = jnp.minimum(b["s2"] + UNITS, recv_at + UNITS)
    below_w1 = b["w1"] > first
    first_b = jnp.where(below_w1, first, jnp.maximum(first, b["w1"] + UNITS))
    last_b = jnp.where(below_w1, jnp.minimum(last, b["w1"]), last)
    return dict(
        is_odd=is_odd,
        near=odd,
        far=1 - odd,
        send_at=pick(b["w3"], b["w1"]),
        recv_at=recv_at,
        first=pick(first, first_b),
        last=pick(last, last_b),
        extra_send=pick(b["low"], mid),
        extra_recv=pick(mid, b["low"]),
        extra_count=pick(other, b["half"]) * exists,
        keep_far_near=pick(b["m1"], b["m3"]) * exists,
        keep_near_far=pick(b["m3"], b["m1"]) * exists,
        keep_near=b["m2"] * exists,
    )


def lanes(unit, count=1):
    return pl.ds(pl.multiple_of(unit * DSTEP, DSTEP), count * DSTEP)


def times(left, right):
    return lax.dot_general(left, right, (((1,), (1,)), ((), ())), preferred_element_type=jnp.float32)


def run(copies):
    for c in copies:
        c.start()
    for c in copies:
        c.wait()


def screen_kernel(n, pair_mask, dom_start, out):
    me = lax.axis_index("wide")
    row = lax.broadcasted_iota(jnp.int32, out.shape, 0)
    column = lax.broadcasted_iota(jnp.int32, out.shape, 1)
    value = jnp.zeros(out.shape, jnp.int32)
    for at in range(PER):
        source = pair_mask if at < PER // 2 else dom_start
        block, r = divmod(at % (PER // 2), 3)
        value = jnp.where(column == at, source[block, r], value)
    out[...] = jnp.where(row == me, value, 0)


def swapped(values):
    return jnp.swapaxes(values, 0, 1)


def pack_kernel(n, screen, bfac, main, extra, level, raw, sems):
    plan = slow_plan(screen, n)
    total = bfac.shape[3] // DSTEP
    near, at = plan["near"], plan["send_at"]
    parts = sems.shape[0]
    step = bfac.shape[1] // parts
    loads = [
        pltpu.make_async_copy(bfac.at[near, pl.ds(q * step, step)], raw.at[pl.ds(q * step, step)], sems.at[q])
        for q in range(parts)
    ]
    for c in loads:
        c.start()
    largest = lax.fori_loop(
        0,
        n // 2 - 1,
        lambda i, most: jnp.maximum(most, boundary(screen, 2 * i + 1)["half"]),
        jnp.int32(0),
    )
    level[0] = sum((largest > c).astype(jnp.int32) for c in LEVELS[:-1])
    for q in range(parts):
        loads[q].wait()
        rows = pl.ds(q * step, step)
        main[:, rows, :] = swapped(raw[rows, :, lanes(at, UNITS)])

    def one(u, carry):
        unit = jnp.minimum(plan["extra_send"] + u, total - 1)
        extra[u] = swapped(raw[:, :, lanes(unit)])
        return carry

    lax.fori_loop(0, SPARE, one, 0)


def inner_kernel(
    n, screen, bfac, other, kband, kmirror, far, near, near_extra, mine, theirs, raw, out, sems
):
    me = lax.axis_index("wide")
    is_odd = lax.rem(me, 2) == 1
    total = bfac.shape[3] // DSTEP
    sources = [(bfac, 0, mine), (bfac, 1, mine), (other, 0, theirs), (other, 1, theirs)]
    loads = [
        pltpu.make_async_copy(source.at[b], raw.at[k % 2], sems.at[k]) for k, (source, b, _) in enumerate(sources)
    ]
    step = 32

    def relayout(k):
        _, b, target = sources[k]
        loads[k].wait()

        def some(q, carry):
            rows = pl.ds(pl.multiple_of(q * step, step), step)
            target[b, :, rows, :] = swapped(raw[k % 2, rows])
            return carry

        lax.fori_loop(0, bfac.shape[1] // step, some, 0)
        if k + 2 < len(loads):
            loads[k + 2].start()

    loads[0].start()
    loads[1].start()

    def product(left, a, right, b, at, keep):
        value = sum(times(left[a, i, :, lanes(at, UNITS)], right[b, i, :, lanes(at, UNITS)]) for i in range(2))
        return value * keep.astype(jnp.float32)

    stores = []

    def store(slot, value, ref, index):
        out[slot] = value
        c = pltpu.make_async_copy(out.at[slot], ref.at[index], sems.at[4 + slot])
        c.start()
        stores.append(c)

    relayout(0)
    relayout(1)
    k, s = flags(screen, me, 0, 0)
    store(0, product(mine, 0, mine, 0, s, k), kband, (0, 0))
    k, s = flags(screen, me, 0, 1)
    value = product(mine, 0, mine, 1, s, k)
    store(1, value, kband, (0, 1))
    store(2, value.T, kmirror, (1, 0))
    k, s = flags(screen, me, 1, 0)
    store(3, product(mine, 1, mine, 1, s, k), kband, (1, 0))

    plan = slow_plan(screen, n)
    window = lanes(plan["recv_at"], UNITS)
    unit = plan["recv_at"] + lax.shift_right_logical(
        lax.broadcasted_iota(jnp.int32, (1, DOM), 1), DSTEP.bit_length() - 1
    )
    counts = jnp.where((unit >= plan["first"]) & (unit < plan["last"]), 1.0, 0.0).astype(near.dtype)
    for i in range(2):
        far[i] = mine[plan["far"], i, :, window]
        near[i] = mine[plan["near"], i, :, window] * counts
        for u in range(SPARE):
            near_extra[u, i] = mine[plan["near"], i, :, lanes(jnp.minimum(plan["extra_recv"] + u, total - 1))]

    relayout(2)
    relayout(3)
    lower = jnp.where(is_odd, me - 1, me)
    b = boundary(screen, lower)
    close = jnp.where(is_odd, 0, 1)
    pick = lambda x, y: jnp.where(is_odd, x, y)
    out[4] = product(mine, 1 - close, theirs, 1 - close, pick(b["s3"], b["s1"]), pick(b["m3"], b["m1"]))
    out[5] = product(mine, close, theirs, 1 - close, b["s2"], b["m2"])
    out[6] = product(mine, close, theirs, close, pick(b["s1"], b["s3"]), pick(b["m1"], b["m3"]))

    def put(targets):
        run([pltpu.make_async_copy(out.at[4 + j], ref, sems.at[8 + j]) for j, ref in enumerate(targets)])

    @pl.when(is_odd)
    def _():
        put([kmirror.at[1, 1], kmirror.at[0, 0], kmirror.at[0, 1]])

    @pl.when(jnp.logical_not(is_odd))
    def _():
        put([kband.at[0, 2], kband.at[1, 1], kband.at[1, 2]])

    for c in stores:
        c.wait()


def extra_kernel(n, screen, near_extra, got, out):
    out[...] = jnp.zeros(out.shape, out.dtype)

    def more(u, carry):
        out[...] += times(near_extra[u, 0], got[u, 0]) + times(near_extra[u, 1], got[u, 1])
        return carry

    lax.fori_loop(0, slow_plan(screen, n)["extra_count"], more, 0)


def slow_kernel(n, got, far, near, extra, far_near, partial, back):
    value = times(far[0], got[0]) + times(far[1], got[1])
    far_near[...] = value
    back[0] = value.T
    value = extra[...] + times(near[0], got[0]) + times(near[1], got[1])
    partial[...] = value
    back[1] = value.T


def last_kernel(n, screen, far_near, partial, back, kband_in, kmirror_in, kband, kmirror, out, sems):
    plan = slow_plan(screen, n)
    out[0] = (partial[...] + back[1]) * plan["keep_near"].astype(jnp.float32)
    out[1] = back[0] * plan["keep_near_far"].astype(jnp.float32)
    out[2] = far_near[...] * plan["keep_far_near"].astype(jnp.float32)

    def put(targets):
        run([pltpu.make_async_copy(out.at[j], ref, sems.at[j]) for j, ref in enumerate(targets)])

    @pl.when(plan["is_odd"])
    def _():
        put([kband.at[1, 1], kband.at[1, 2], kband.at[0, 2]])

    @pl.when(jnp.logical_not(plan["is_odd"]))
    def _():
        put([kmirror.at[0, 0], kmirror.at[0, 1], kmirror.at[1, 1]])


def call(kernel, n, outs, ins, out_specs, scratch, flops, bytes_moved, aliases=None, vmem=40):
    return pl.pallas_call(
        functools.partial(kernel, n),
        out_shape=outs,
        in_specs=ins,
        out_specs=out_specs,
        scratch_shapes=scratch,
        input_output_aliases=aliases or {},
        compiler_params=pltpu.CompilerParams(vmem_limit_bytes=vmem * 2**20),
        cost_estimate=pl.CostEstimate(flops=flops, bytes_accessed=bytes_moved, transcendentals=0),
        name=kernel.__name__,
    )


def per_device(bfac, pair_mask, dom_start):
    n = lax.axis_size("wide")
    _, rows, orbitals, fitting = bfac.shape
    slow = [p for i in range(1, n - 1, 2) for p in ((i, i + 1), (i + 1, i))]
    fast = [p for i in range(0, n, 2) for p in ((i, i + 1), (i + 1, i))]
    f32, bf16 = jnp.float32, bfac.dtype
    shape = jax.ShapeDtypeStruct
    dma = pltpu.SemaphoreType.DMA

    own = call(screen_kernel, n, shape((n, 128), jnp.int32), [SMEM, SMEM], VMEM, [], 0, 2**14)(pair_mask, dom_start)
    screen = lax.psum(own, "wide")

    window = shape((orbitals, rows, DOM), bf16)
    spare = shape((SPARE, orbitals, rows, DSTEP), bf16)
    main, extra, level = call(
        pack_kernel,
        n,
        (window, spare, shape((1,), jnp.int32)),
        [SMEM, HBM],
        (VMEM, VMEM, SMEM),
        [pltpu.VMEM((rows, orbitals, fitting), bf16), dma((4,))],
        0,
        6 * 2**20,
        vmem=60,
    )(screen, bfac)
    main_got = lax.ppermute(main, "wide", slow)

    band = shape((2, 3, rows, rows), f32)
    mirror = shape((2, 2, rows, rows), f32)
    square = shape((rows, rows), f32)
    inner_outs = (band, mirror, window, window, spare)

    def inner(screen, bfac):
        other = lax.ppermute(bfac, "wide", fast)
        return call(
            inner_kernel,
            n,
            inner_outs,
            [SMEM, HBM, HBM],
            (HBM, HBM, VMEM, VMEM, VMEM),
            [
                pltpu.VMEM((2, orbitals, rows, fitting), bf16),
                pltpu.VMEM((2, orbitals, rows, fitting), bf16),
                pltpu.VMEM((2, rows, orbitals, fitting), bf16),
                pltpu.VMEM((7, rows, rows), f32),
                dma((11,)),
            ],
            12 * rows * rows * orbitals * DOM,
            25 * 2**20,
            vmem=52,
        )(screen, bfac, other)

    def unused(screen, bfac):
        return tuple(jnp.zeros(o.shape, o.dtype) for o in inner_outs)

    kband, kmirror, far, near, near_extra = lax.cond(level[0] >= 0, inner, unused, screen, bfac)
    def extras(count):
        def branch(screen, extra, near_extra):
            if count == 0:
                return jnp.zeros((rows, rows), f32)
            got = lax.ppermute(extra[:count], "wide", slow)
            return call(extra_kernel, n, square, [SMEM, VMEM, VMEM], VMEM, [], 2**26 * count, 2**19 * count)(
                screen, near_extra, got
            )

        return branch

    more = lax.switch(level[0], [extras(c) for c in LEVELS], screen, extra, near_extra)

    far_near, partial, back = call(
        slow_kernel,
        n,
        (square, square, shape((2, rows, rows), f32)),
        [VMEM] * 4,
        (VMEM, VMEM, VMEM),
        [],
        4 * rows * rows * orbitals * DOM,
        8 * 2**20,
    )(main_got, far, near, more)
    back_got = lax.ppermute(back, "wide", slow)
    return call(
        last_kernel,
        n,
        (band, mirror),
        [SMEM, VMEM, VMEM, VMEM, HBM, HBM],
        (HBM, HBM),
        [pltpu.VMEM((3, rows, rows), f32), dma((3,))],
        0,
        2**21,
        {4: 0, 5: 1},
    )(screen, far_near, partial, back_got, kband, kmirror)


def solution(mesh):
    placed = (P("wide", None, "groups", None), P("wide", None), P("wide", None))
    return jax.shard_map(
        per_device,
        mesh=mesh,
        in_specs=placed,
        out_specs=(
            P(("groups", "wide"), None, None, None),
            P(("groups", "wide"), None, None, None),
        ),
        check_vma=False,
    )
```

profile of v0, /device:TPU:9, one launch (start us, length us, event | category | flops | bytes accessed | tf_op | source)
XLA Modules:
  0.0 92.4 jit_solution(8106302394870053888)
XLA Ops:
  0.6 0.0 copy-start
  0.6 0.7 copy-done
  1.3 0.0 copy-start.1
  1.3 0.7 copy-done.1
  2.0 0.6 screen_kernel.1
  2.6 8.9 %psum.7.screen = s32[16,128]{1,0:T(8,128)S(1)} all-reduce(s32[16,128]{1,0:T(8,128)S(1)} %screen_kernel.1), channel_id=1, replica_groups=mesh['groups'=2,'wide'=16] {'wide'}, use_global_device_ids=true, to_apply=%region_0.0 | all-reduce | flops 2048 | bytes 16384 | tf_op jit(solution)/shard_map/psum | solution.py:288
  11.5 7.0 %pack_kernel.1 = (bf16[2,256,2048]{2,1,0:T(8,128)(2,1)}, bf16[8,2,256,128]{3,2,1,0:T(8,128)(2,1)}, s32[1]{0:T(128)}) custom-call(s32[16,128]{1,0:T(8,128)S(1)} %psum.7.screen, bf16[2,256,2,4096]{3,2,1,0:T(2,128)(2,1)} %bfac.1), custom_call_target="tpu_custom_call" | custom-call | bytes 6291456 | tf_op jit(solution)/shard_map/pack_kernel/pallas_call | solution.py:292
  18.5 5.4 %collective-permute-start.7 = (bf16[2,256,2048]{2,1,0:T(8,128)(2,1)}, bf16[2,256,2048]{2,1,0:T(8,128)(2,1)S(1)}, u32[]{:S(2)}, u32[]{:S(2)}) collective-permute-start(bf16[2,256,2048]{2,1,0:T(8,128)(2,1)} %get-tuple-element.81), channel_id=1, source_target_pairs={{1,2},{2,1},{3,4},{4,3},{5,6},{6,5},{7,8},{8,7},{9,10},{10,9},{11,... | collective-permute-start | bytes 6291464 | tf_op jit(solution)/shard_map/ppermute | solution.py:303
  25.2 31.6 %conditional.2 = ((f32[2,3,256,256]{3,2,1,0:T(8,128)}, f32[2,2,256,256]{3,2,1,0:T(8,128)}, bf16[2,256,2048]{2,1,0:T(8,128)(2,1)}, bf16[2,256,2048]{2,1,0:T(8,128)(2,1)}, bf16[8,2,256,128]{3,2,1,0:T(8,128)(2,1)S(1)})) conditional(s32[]{:T(128)} %bitcast, () %tuple.35, (bf16[2,256,2,4096]{3,2,1,0:T(2,128)(2,1)}, s32[16,128]{1,0:T(8,128)S(1)}) %tuple.36), branch_computations={%region_1.0_spmd, %region_2.0_spmd} | conditional | flops 3221225472 | bytes 93323336 | solution.py:333
  25.2 0.1 collective-permute-start
  25.3 13.4 %collective-permute-done.other = bf16[2,256,2,4096]{3,2,1,0:T(2,128)(2,1)S(1)} collective-permute-done((bf16[2,256,2,4096]{3,2,1,0:T(2,128)(2,1)}, bf16[2,256,2,4096]{3,2,1,0:T(2,128)(2,1)S(1)}, u32[]{:S(2)}, u32[]{:S(2)}) %collective-permute-start) | collective-permute-done | bytes 8388640 | tf_op jit(solution)/shard_map/cond/branch_1_fun/ppermute | solution.py:311
  38.7 0.0 copy-start.2
  38.7 3.2 %copy-done.2 = bf16[2,256,2,4096]{3,2,1,0:T(2,128)(2,1)} copy-done((bf16[2,256,2,4096]{3,2,1,0:T(2,128)(2,1)}, bf16[2,256,2,4096]{3,2,1,0:T(2,128)(2,1)S(1)}, u32[]{:S(2)}) %copy-start.2) | copy-done | bytes 8388632 | tf_op jit(solution)/shard_map/cond
  41.9 14.9 %inner_kernel.1 = (f32[2,3,256,256]{3,2,1,0:T(8,128)}, f32[2,2,256,256]{3,2,1,0:T(8,128)}, bf16[2,256,2048]{2,1,0:T(8,128)(2,1)}, bf16[2,256,2048]{2,1,0:T(8,128)(2,1)}, bf16[8,2,256,128]{3,2,1,0:T(8,128)(2,1)S(1)}) custom-call(s32[16,128]{1,0:T(8,128)S(1)} %get-tuple-element.40.screen, bf16[2,256,2,4096]{3,2,1,0:T(2,128)(2,1)} %get-tuple-element.41.bfac, ...), custom_call_target="tpu_custom_call" | custom-call | flops 3221225472 | bytes 26214400 | tf_op jit(solution)/shard_map/cond/branch_1_fun/inner_kernel/pallas_call | solution.py:312
  56.8 19.8 %conditional.3 = (f32[256,256]{1,0:T(8,128)S(1)}) conditional(s32[]{:T(128)} %bitcast.1, () %tuple.37, (bf16[8,2,256,128]{3,2,1,0:T(8,128)(2,1)}, s32[16,128]{1,0:T(8,128)S(1)}, bf16[8,2,256,128]{3,2,1,0:T(8,128)(2,1)S(1)}) %tuple.38, (bf16[8,2,256,128]{3,2,1,0:T(8,128)(2,1)}, s32[16,128]{1,0:T(8,128)S(1)}, ...), branch_computations={%region_3.0_spmd, %region_4.0_spmd, %region_5.0_spmd, %region_6.0_... | conditional | flops 536870912 | bytes 8388656 | solution.py:345
  56.8 1.0 %slice.11 = bf16[2,2,256,128]{3,2,1,0:T(8,128)(2,1)S(1)} slice(bf16[8,2,256,128]{3,2,1,0:T(8,128)(2,1)} %get-tuple-element.55), slice={[0:2], [0:2], [0:256], [0:128]} | slice | bytes 524288 | tf_op jit(solution)/shard_map/cond/branch_2_fun/slice | solution.py:338
  57.8 2.7 %collective-permute-start.2 = (bf16[2,2,256,128]{3,2,1,0:T(8,128)(2,1)S(1)}, bf16[2,2,256,128]{3,2,1,0:T(8,128)(2,1)S(1)}, u32[]{:S(2)}, u32[]{:S(2)}) collective-permute-start(bf16[2,2,256,128]{3,2,1,0:T(8,128)(2,1)S(1)} %slice.11), channel_id=1, source_target_pairs={{1,2},{2,1},{3,4},{4,3},{5,6},{6,5},{7,8},{8,7},{9,10},{10,9},{11,... | collective-permute-start | bytes 786440 | tf_op jit(solution)/shard_map/cond/branch_2_fun/ppermute | solution.py:338
  60.5 15.4 %collective-permute-done.2.got = bf16[2,2,256,128]{3,2,1,0:T(8,128)(2,1)S(1)} collective-permute-done((bf16[2,2,256,128]{3,2,1,0:T(8,128)(2,1)S(1)}, bf16[2,2,256,128]{3,2,1,0:T(8,128)(2,1)S(1)}, u32[]{:S(2)}, u32[]{:S(2)}) %collective-permute-start.2) | collective-permute-done | bytes 262176 | tf_op jit(solution)/shard_map/cond/branch_2_fun/ppermute | solution.py:338
  75.9 0.7 extra_kernel.7
  76.6 0.0 collective-permute-done.7.got
  76.7 3.6 %slow_kernel.1 = (f32[256,256]{1,0:T(8,128)S(1)}, f32[256,256]{1,0:T(8,128)S(1)}, f32[2,256,256]{2,1,0:T(8,128)S(1)}) custom-call(bf16[2,256,2048]{2,1,0:T(8,128)(2,1)S(1)} %collective-permute-done.7.got, bf16[2,256,2048]{2,1,0:T(8,128)(2,1)} %get-tuple-element.83.far, bf16[2,256,2048]{2,1,0:T(8,128)(2,1)} %get-tuple-element.84.near, ...), custom_call_target="tpu_custom_call" | custom-call | flops 1073741824 | bytes 8388608 | tf_op jit(solution)/shard_map/slow_kernel/pallas_call | solution.py:347
  80.3 3.3 %collective-permute-start.8 = (f32[2,256,256]{2,1,0:T(8,128)S(1)}, f32[2,256,256]{2,1,0:T(8,128)S(1)}, u32[]{:S(2)}, u32[]{:S(2)}) collective-permute-start(f32[2,256,256]{2,1,0:T(8,128)S(1)} %get-tuple-element.89), channel_id=1, source_target_pairs={{1,2},{2,1},{3,4},{4,3},{5,6},{6,5},{7,8},{8,7},{9,10},{10,9},{11,... | collective-permute-start | bytes 1572872 | tf_op jit(solution)/shard_map/ppermute | solution.py:357
  83.6 7.2 %collective-permute-done.8.back = f32[2,256,256]{2,1,0:T(8,128)S(1)} collective-permute-done((f32[2,256,256]{2,1,0:T(8,128)S(1)}, f32[2,256,256]{2,1,0:T(8,128)S(1)}, u32[]{:S(2)}, u32[]{:S(2)}) %collective-permute-start.8) | collective-permute-done | bytes 524320 | tf_op jit(solution)/shard_map/ppermute | solution.py:357
  90.8 1.6 %last_kernel.1 = (f32[2,3,256,256]{3,2,1,0:T(8,128)}, f32[2,2,256,256]{3,2,1,0:T(8,128)}) custom-call(s32[16,128]{1,0:T(8,128)S(1)} %psum.7.screen, f32[256,256]{1,0:T(8,128)S(1)} %get-tuple-element.87.far_near, f32[256,256]{1,0:T(8,128)S(1)} %get-tuple-element.88.partial, ...), custom_call_target="tpu_custom_call", output_to_operand_aliasing={{0}: (4, {}), {1}: (5, {})} | custom-call | bytes 2097152 | tf_op jit(solution)/shard_map/last_kernel/pallas_call | solution.py:358
Async XLA Ops:
  0.6 0.7 copy-start
  1.3 0.7 copy-start.1
  18.5 58.2 %collective-permute-start.7 = (bf16[2,256,2048]{2,1,0:T(8,128)(2,1)}, bf16[2,256,2048]{2,1,0:T(8,128)(2,1)S(1)}, u32[]{:S(2)}, u32[]{:S(2)}) collective-permute-start(bf16[2,256,2048]{2,1,0:T(8,128)(2,1)} %get-tuple-element.81), channel_id=1, source_target_pairs={{1,2},{2,1},{3,4},{4,3},{5,6},{6,5},{7,8},{8,7},{9,10},{10,9},{11,... | collective-permute-start | bytes 6291464 | tf_op jit(solution)/shard_map/ppermute | solution.py:303
  25.2 13.4 %collective-permute-start = (bf16[2,256,2,4096]{3,2,1,0:T(2,128)(2,1)}, bf16[2,256,2,4096]{3,2,1,0:T(2,128)(2,1)S(1)}, u32[]{:S(2)}, u32[]{:S(2)}) collective-permute-start(bf16[2,256,2,4096]{3,2,1,0:T(2,128)(2,1)} %get-tuple-element.41.bfac), channel_id=1, source_target_pairs={{0,1},{1,0},{2,3},{3,2},{4,5},{5,4},{6,7},{7,6},{8,9},{9,8},{10,11... | collective-permute-start | bytes 25165832 | tf_op jit(solution)/shard_map/cond/branch_1_fun/ppermute | solution.py:311
  38.7 3.2 %copy-start.2 = (bf16[2,256,2,4096]{3,2,1,0:T(2,128)(2,1)}, bf16[2,256,2,4096]{3,2,1,0:T(2,128)(2,1)S(1)}, u32[]{:S(2)}) copy-start(bf16[2,256,2,4096]{3,2,1,0:T(2,128)(2,1)S(1)} %collective-permute-done.other) | copy-start | bytes 25165828 | tf_op jit(solution)/shard_map/cond
  57.8 18.1 %collective-permute-start.2 = (bf16[2,2,256,128]{3,2,1,0:T(8,128)(2,1)S(1)}, bf16[2,2,256,128]{3,2,1,0:T(8,128)(2,1)S(1)}, u32[]{:S(2)}, u32[]{:S(2)}) collective-permute-start(bf16[2,2,256,128]{3,2,1,0:T(8,128)(2,1)S(1)} %slice.11), channel_id=1, source_target_pairs={{1,2},{2,1},{3,4},{4,3},{5,6},{6,5},{7,8},{8,7},{9,10},{10,9},{11,... | collective-permute-start | bytes 786440 | tf_op jit(solution)/shard_map/cond/branch_2_fun/ppermute | solution.py:338
  80.3 10.5 %collective-permute-start.8 = (f32[2,256,256]{2,1,0:T(8,128)S(1)}, f32[2,256,256]{2,1,0:T(8,128)S(1)}, u32[]{:S(2)}, u32[]{:S(2)}) collective-permute-start(f32[2,256,256]{2,1,0:T(8,128)S(1)} %get-tuple-element.89), channel_id=1, source_target_pairs={{1,2},{2,1},{3,4},{4,3},{5,6},{6,5},{7,8},{8,7},{9,10},{10,9},{11,... | collective-permute-start | bytes 1572872 | tf_op jit(solution)/shard_map/ppermute | solution.py:357
where the time goes:
time: 93.9 us; the launch traced here: 92.4 us
  waiting for transfers between devices  36 us (38%)
  Pallas kernels  28.4 us (30%)
  starting transfers between devices  11.5 us (12%)
  blocking collectives  8.92 us (9%)
  local copies, waits for them, and re-layouts  5.55 us (6%)
  between operations  2.01 us (2%)
    ppermute x1, waiting for transfers between devices, branch(): got = lax.ppermute(extra[:count], 'wide', slow)  15.4 us
    pallas_call x1, Pallas kernels, inner(): call(inner_kernel, n, inner_outs, [SMEM, HBM, HBM], (HBM, HBM, VMEM, VMEM...  14.9 us
    ppermute x1, waiting for transfers between devices, inner(): other = lax.ppermute(bfac, 'wide', fast)  13.4 us
    psum x1, blocking collectives, per_device(): screen = lax.psum(own, 'wide')  8.92 us
    ppermute x1, waiting for transfers between devices, per_device(): back_got = lax.ppermute(back, 'wide', slow)  7.22 us
    pallas_call x1, Pallas kernels, per_device(): call(pack_kernel, n, (window, spare, shape((1,), jnp.int32)), [SMEM, HBM]...  6.97 us
    ppermute x1, starting transfers between devices, per_device(): main_got = lax.ppermute(main, 'wide', slow)  5.45 us
    pallas_call x1, Pallas kernels, per_device(): call(slow_kernel, n, (square, square, shape((2, rows, rows), f32)), [VMEM...  3.63 us
  transfers between devices with their start and end apart: 4, of which 3 were waited for; matrix products, arithmetic and copies ran while one was open for 1% of the time, Pallas kernels for 17%

commit v1 on v0

--- a/solution.py
+++ b/solution.py
@@ -18,15 +18,19 @@
 HBM = pl.BlockSpec(memory_space=pltpu.HBM)
 
 
-def flags(screen, device, block, r):
+def flags(screen, block, r, row=0):
     at = block * 3 + r
-    return screen[device, at], screen[device, at + PER // 2]
-
-
-def boundary(screen, device):
-    m1, s1 = flags(screen, device, 0, 2)
-    m2, s2 = flags(screen, device, 1, 1)
-    m3, s3 = flags(screen, device, 1, 2)
+    return screen[row, at], screen[row, at + PER // 2]
+
+
+def choose(is_first, first, second):
+    return tuple(jnp.where(is_first, a, b) for a, b in zip(first, second))
+
+
+def boundary(get):
+    m1, s1 = get(0, 2)
+    m2, s2 = get(1, 1)
+    m3, s3 = get(1, 2)
     w1 = jnp.where(m1 > 0, s1, s2)
     w3 = jnp.where(m3 > 0, s3, s2)
     low, high = s2, s2 + UNITS
@@ -40,13 +44,12 @@
     return dict(m1=m1, s1=s1, m2=m2, s2=s2, m3=m3, s3=s3, w1=w1, w3=w3, low=low, half=half, rest=rest)
 
 
-def slow_plan(screen, n):
+def slow_plan(own, below, n):
     me = lax.axis_index("wide")
     odd = lax.rem(me, 2)
     is_odd = odd == 1
-    lower = jnp.where(is_odd, me, jnp.maximum(me - 1, 0))
     exists = jnp.where(is_odd, me < n - 1, me > 0).astype(jnp.int32)
-    b = boundary(screen, lower)
+    b = boundary(lambda block, r: choose(is_odd, flags(own, block, r), flags(below, block, r)))
     pick = lambda a, c: jnp.where(is_odd, a, c)
     mid = b["low"] + b["half"]
     other = b["rest"] - b["half"]
@@ -88,25 +91,32 @@
         c.wait()
 
 
-def screen_kernel(n, pair_mask, dom_start, out):
-    me = lax.axis_index("wide")
-    row = lax.broadcasted_iota(jnp.int32, out.shape, 0)
+def screen_kernel(n, pair_mask, dom_start, out, again, sem):
     column = lax.broadcasted_iota(jnp.int32, out.shape, 1)
     value = jnp.zeros(out.shape, jnp.int32)
     for at in range(PER):
         source = pair_mask if at < PER // 2 else dom_start
         block, r = divmod(at % (PER // 2), 3)
         value = jnp.where(column == at, source[block, r], value)
-    out[...] = jnp.where(row == me, value, 0)
+    out[...] = value
+    run([pltpu.make_async_copy(out, again, sem)])
+
+
+def level_kernel(n, screens, level):
+    def one(i, most):
+        row = (2 * i + 1) * 8
+        return jnp.maximum(most, boundary(lambda block, r: flags(screens, block, r, row))["half"])
+
+    largest = lax.fori_loop(0, n // 2 - 1, one, jnp.int32(0))
+    level[0] = sum((largest > c).astype(jnp.int32) for c in LEVELS[:-1])
 
 
 def swapped(values):
     return jnp.swapaxes(values, 0, 1)
 
 
-def pack_kernel(n, screen, bfac, main, extra, level, raw, sems):
-    plan = slow_plan(screen, n)
-    total = bfac.shape[3] // DSTEP
+def pack_kernel(n, own, below, bfac, main, raw, sems):
+    plan = slow_plan(own, below, n)
     near, at = plan["near"], plan["send_at"]
     parts = sems.shape[0]
     step = bfac.shape[1] // parts
@@ -116,28 +126,14 @@
     ]
     for c in loads:
         c.start()
-    largest = lax.fori_loop(
-        0,
-        n // 2 - 1,
-        lambda i, most: jnp.maximum(most, boundary(screen, 2 * i + 1)["half"]),
-        jnp.int32(0),
-    )
-    level[0] = sum((largest > c).astype(jnp.int32) for c in LEVELS[:-1])
     for q in range(parts):
         loads[q].wait()
         rows = pl.ds(q * step, step)
         main[:, rows, :] = swapped(raw[rows, :, lanes(at, UNITS)])
 
-    def one(u, carry):
-        unit = jnp.minimum(plan["extra_send"] + u, total - 1)
-        extra[u] = swapped(raw[:, :, lanes(unit)])
-        return carry
-
-    lax.fori_loop(0, SPARE, one, 0)
-
 
 def inner_kernel(
-    n, screen, bfac, other, kband, kmirror, far, near, near_extra, mine, theirs, raw, out, sems
+    n, own, below, bfac, other, kband, kmirror, far, near, near_extra, extra, mine, theirs, raw, out, sems
 ):
     me = lax.axis_index("wide")
     is_odd = lax.rem(me, 2) == 1
@@ -178,16 +174,16 @@
 
     relayout(0)
     relayout(1)
-    k, s = flags(screen, me, 0, 0)
+    k, s = flags(own, 0, 0)
     store(0, product(mine, 0, mine, 0, s, k), kband, (0, 0))
-    k, s = flags(screen, me, 0, 1)
+    k, s = flags(own, 0, 1)
     value = product(mine, 0, mine, 1, s, k)
     store(1, value, kband, (0, 1))
     store(2, value.T, kmirror, (1, 0))
-    k, s = flags(screen, me, 1, 0)
+    k, s = flags(own, 1, 0)
     store(3, product(mine, 1, mine, 1, s, k), kband, (1, 0))
 
-    plan = slow_plan(screen, n)
+    plan = slow_plan(own, below, n)
     window = lanes(plan["recv_at"], UNITS)
     unit = plan["recv_at"] + lax.shift_right_logical(
         lax.broadcasted_iota(jnp.int32, (1, DOM), 1), DSTEP.bit_length() - 1
@@ -198,11 +194,11 @@
         near[i] = mine[plan["near"], i, :, window] * counts
         for u in range(SPARE):
             near_extra[u, i] = mine[plan["near"], i, :, lanes(jnp.minimum(plan["extra_recv"] + u, total - 1))]
+            extra[u, i] = mine[plan["near"], i, :, lanes(jnp.minimum(plan["extra_send"] + u, total - 1))]
 
     relayout(2)
     relayout(3)
-    lower = jnp.where(is_odd, me - 1, me)
-    b = boundary(screen, lower)
+    b = boundary(lambda block, r: choose(is_odd, flags(below, block, r), flags(own, block, r)))
     close = jnp.where(is_odd, 0, 1)
     pick = lambda x, y: jnp.where(is_odd, x, y)
     out[4] = product(mine, 1 - close, theirs, 1 - close, pick(b["s3"], b["s1"]), pick(b["m3"], b["m1"]))
@@ -224,14 +220,14 @@
         c.wait()
 
 
-def extra_kernel(n, screen, near_extra, got, out):
+def extra_kernel(n, own, below, near_extra, got, out):
     out[...] = jnp.zeros(out.shape, out.dtype)
 
     def more(u, carry):
         out[...] += times(near_extra[u, 0], got[u, 0]) + times(near_extra[u, 1], got[u, 1])
         return carry
 
-    lax.fori_loop(0, slow_plan(screen, n)["extra_count"], more, 0)
+    lax.fori_loop(0, slow_plan(own, below, n)["extra_count"], more, 0)
 
 
 def slow_kernel(n, got, far, near, extra, far_near, partial, back):
@@ -243,8 +239,8 @@
     back[1] = value.T
 
 
-def last_kernel(n, screen, far_near, partial, back, kband_in, kmirror_in, kband, kmirror, out, sems):
-    plan = slow_plan(screen, n)
+def last_kernel(n, own, below, far_near, partial, back, kband_in, kmirror_in, kband, kmirror, out, sems):
+    plan = slow_plan(own, below, n)
     out[0] = (partial[...] + back[1]) * plan["keep_near"].astype(jnp.float32)
     out[1] = back[0] * plan["keep_near_far"].astype(jnp.float32)
     out[2] = far_near[...] * plan["keep_far_near"].astype(jnp.float32)
@@ -284,37 +280,41 @@
     shape = jax.ShapeDtypeStruct
     dma = pltpu.SemaphoreType.DMA
 
-    own = call(screen_kernel, n, shape((n, 128), jnp.int32), [SMEM, SMEM], VMEM, [], 0, 2**14)(pair_mask, dom_start)
-    screen = lax.psum(own, "wide")
-
     window = shape((orbitals, rows, DOM), bf16)
     spare = shape((SPARE, orbitals, rows, DSTEP), bf16)
-    main, extra, level = call(
+    ints = shape((8, 128), jnp.int32)
+    own, again = call(screen_kernel, n, (ints, ints), [SMEM, SMEM], (VMEM, HBM), [dma(())], 0, 2**14, vmem=60)(
+        pair_mask, dom_start
+    )
+    below = lax.ppermute(own, "wide", [(i, i + 1) for i in range(n - 1)])
+    screens = lax.all_gather(again, "wide", tiled=True)
+
+    main = call(
         pack_kernel,
         n,
-        (window, spare, shape((1,), jnp.int32)),
-        [SMEM, HBM],
-        (VMEM, VMEM, SMEM),
+        window,
+        [SMEM, SMEM, HBM],
+        VMEM,
         [pltpu.VMEM((rows, orbitals, fitting), bf16), dma((4,))],
         0,
         6 * 2**20,
         vmem=60,
-    )(screen, bfac)
+    )(own, below, bfac)
     main_got = lax.ppermute(main, "wide", slow)
 
     band = shape((2, 3, rows, rows), f32)
     mirror = shape((2, 2, rows, rows), f32)
     square = shape((rows, rows), f32)
-    inner_outs = (band, mirror, window, window, spare)
-
-    def inner(screen, bfac):
+    inner_outs = (band, mirror, window, window, spare, spare)
+
+    def inner(own, below, bfac):
         other = lax.ppermute(bfac, "wide", fast)
         return call(
             inner_kernel,
             n,
             inner_outs,
-            [SMEM, HBM, HBM],
-            (HBM, HBM, VMEM, VMEM, VMEM),
+            [SMEM, SMEM, HBM, HBM],
+            (HBM, HBM, VMEM, VMEM, VMEM, VMEM),
             [
                 pltpu.VMEM((2, orbitals, rows, fitting), bf16),
                 pltpu.VMEM((2, orbitals, rows, fitting), bf16),
@@ -325,24 +325,27 @@
             12 * rows * rows * orbitals * DOM,
             25 * 2**20,
             vmem=52,
-        )(screen, bfac, other)
-
-    def unused(screen, bfac):
+        )(own, below, bfac, other)
+
+    def unused(own, below, bfac):
         return tuple(jnp.zeros(o.shape, o.dtype) for o in inner_outs)
 
-    kband, kmirror, far, near, near_extra = lax.cond(level[0] >= 0, inner, unused, screen, bfac)
+    level = call(level_kernel, n, shape((1,), jnp.int32), [SMEM], SMEM, [], 0, 2**16)(screens)
+    own, below, bfac, _ = lax.optimization_barrier((own, below, bfac, main))
+    kband, kmirror, far, near, near_extra, extra = lax.cond(level[0] >= 0, inner, unused, own, below, bfac)
+
     def extras(count):
-        def branch(screen, extra, near_extra):
+        def branch(own, below, extra, near_extra):
             if count == 0:
                 return jnp.zeros((rows, rows), f32)
             got = lax.ppermute(extra[:count], "wide", slow)
-            return call(extra_kernel, n, square, [SMEM, VMEM, VMEM], VMEM, [], 2**26 * count, 2**19 * count)(
-                screen, near_extra, got
+            return call(extra_kernel, n, square, [SMEM, SMEM, VMEM, VMEM], VMEM, [], 2**26 * count, 2**19 * count)(
+                own, below, near_extra, got
             )
 
         return branch
 
-    more = lax.switch(level[0], [extras(c) for c in LEVELS], screen, extra, near_extra)
+    more = lax.switch(level[0], [extras(c) for c in LEVELS], own, below, extra, near_extra)
 
     far_near, partial, back = call(
         slow_kernel,
@@ -359,13 +362,13 @@
         last_kernel,
         n,
         (band, mirror),
-        [SMEM, VMEM, VMEM, VMEM, HBM, HBM],
+        [SMEM, SMEM, VMEM, VMEM, VMEM, HBM, HBM],
         (HBM, HBM),
         [pltpu.VMEM((3, rows, rows), f32), dma((3,))],
         0,
         2**21,
-        {4: 0, 5: 1},
-    )(screen, far_near, partial, back_got, kband, kmirror)
+        {5: 0, 6: 1},
+    )(own, below, far_near, partial, back_got, kband, kmirror)
 
 
 def solution(mesh):

time: 93.9 us -> 143 us (1.52)
  blocking collectives: 8.92 us -> 55 us
  starting transfers between devices: 11.5 us -> 16.4 us
  waiting for transfers between devices: 36 us -> 33.7 us
  Pallas kernels: 28.4 us -> 30 us
    all_gather x0 -> x1, blocking collectives: none -> 55 us  [per_device(): screens = lax.all_gather(again, 'wide', tiled=True)]
    psum x1 -> x0, blocking collectives: 8.92 us -> none  [per_device(): screen = lax.psum(own, 'wide')]
    ppermute x1, waiting for transfers between devices: 15.4 us -> 9.66 us  [branch(): got = lax.ppermute(extra[:count], 'wide', slow)]
    ppermute x0 -> x1, starting transfers between devices: none -> 3.68 us  [per_device(): below = lax.ppermute(own, 'wide', [(i, i + 1) for i in range(n - 1)])]
    ppermute x1, waiting for transfers between devices: 7.22 us -> 10.2 us  [per_device(): back_got = lax.ppermute(back, 'wide', slow)]
    ppermute x1, starting transfers between devices: 2.7 us -> 4.47 us  [branch(): got = lax.ppermute(extra[:count], 'wide', slow)]
    pallas_call x5 -> x6, Pallas kernels: 24.8 us -> 26.3 us  [the longest x1 15.4 us: inner(): call(inner_kernel, n, inner_outs, [SMEM, SMEM, HBM, HBM], (HBM, HBM, VMEM...]
  transfers between devices with their start and end apart: 4 -> 5, of which waited for: 3 -> 4; matrix products, arithmetic and copies ran while one was open for 1% -> 1% of each run, Pallas kernels for 17% -> 13%
where the time goes in v1:
time: 143 us; the launch traced here: 141 us
  blocking collectives  55 us (38%)
  waiting for transfers between devices  33.7 us (24%)
  Pallas kernels  30 us (21%)
  starting transfers between devices  16.4 us (11%)
  local copies, waits for them, and re-layouts  4.27 us (3%)
  between operations  2.02 us (1%)
    all_gather x1, blocking collectives, per_device(): screens = lax.all_gather(again, 'wide', tiled=True)  55 us
    pallas_call x1, Pallas kernels, inner(): call(inner_kernel, n, inner_outs, [SMEM, SMEM, HBM, HBM], (HBM, HBM, VMEM...  15.4 us
    ppermute x1, waiting for transfers between devices, inner(): other = lax.ppermute(bfac, 'wide', fast)  13 us
    ppermute x1, waiting for transfers between devices, per_device(): back_got = lax.ppermute(back, 'wide', slow)  10.2 us
    ppermute x1, waiting for transfers between devices, branch(): got = lax.ppermute(extra[:count], 'wide', slow)  9.66 us
    ppermute x1, starting transfers between devices, branch(): got = lax.ppermute(extra[:count], 'wide', slow)  4.47 us
    pallas_call x1, Pallas kernels, per_device(): call(pack_kernel, n, window, [SMEM, SMEM, HBM], VMEM, [pltpu.VMEM((rows,...  4.37 us
    ppermute x1, starting transfers between devices, per_device(): main_got = lax.ppermute(main, 'wide', slow)  4.19 us
  transfers between devices with their start and end apart: 5, of which 4 were waited for; matrix products, arithmetic and copies ran while one was open for 1% of the time, Pallas kernels for 13%

profile of v1, /device:TPU:9, one launch (start us, length us, event | category | flops | bytes accessed | tf_op | source)
XLA Modules:
  0.0 141.4 jit_solution(2426507934768911907)
XLA Ops:
  0.6 1.3 screen_kernel.1
  2.0 0.0 copy-start.1
  2.0 3.7 %collective-permute-start.7 = (s32[8,128]{1,0:T(8,128)S(1)}, s32[8,128]{1,0:T(8,128)S(1)}, u32[]{:S(2)}, u32[]{:S(2)}) collective-permute-start(s32[8,128]{1,0:T(8,128)S(1)} %get-tuple-element.106.own), channel_id=1, source_target_pairs={{0,1},{1,2},{2,3},{3,4},{4,5},{5,6},{6,7},{7,8},{8,9},{9,10},{10,1... | collective-permute-start | bytes 12296 | tf_op jit(solution)/shard_map/ppermute | solution.py:289
  5.7 0.7 collective-permute-done.7.below
  6.4 4.4 %pack_kernel.1 = bf16[2,256,2048]{2,1,0:T(8,128)(2,1)} custom-call(s32[8,128]{1,0:T(8,128)S(1)} %get-tuple-element.106.own, s32[8,128]{1,0:T(8,128)S(1)} %collective-permute-done.7.below, bf16[2,256,2,4096]{3,2,1,0:T(2,128)(2,1)} %bfac.1), custom_call_target="tpu_custom_call" | custom-call | bytes 6291456 | tf_op jit(solution)/shard_map/pack_kernel/pallas_call | solution.py:292
  10.8 4.2 %collective-permute-start.8 = (bf16[2,256,2048]{2,1,0:T(8,128)(2,1)}, bf16[2,256,2048]{2,1,0:T(8,128)(2,1)S(1)}, u32[]{:S(2)}, u32[]{:S(2)}) collective-permute-start(bf16[2,256,2048]{2,1,0:T(8,128)(2,1)} %pack_kernel.1), channel_id=1, source_target_pairs={{1,2},{2,1},{3,4},{4,3},{5,6},{6,5},{7,8},{8,7},{9,10},{10,9},{11,... | collective-permute-start | bytes 6291464 | tf_op jit(solution)/shard_map/ppermute | solution.py:303
  15.0 0.0 copy-done.1
  15.0 55.0 %all_gather.3.screens = s32[128,128]{1,0:T(8,128)S(1)} all-gather(s32[8,128]{1,0:T(8,128)S(1)} %copy-done.1), channel_id=1, replica_groups=mesh['groups'=2,'wide'=16] {'wide'}, dimensions={0}, use_global_device_ids=true | all-gather | bytes 69632 | tf_op jit(solution)/shard_map/all_gather | solution.py:290
  69.9 2.3 %level_kernel.1 = s32[1]{0:T(128)} custom-call(s32[128,128]{1,0:T(8,128)S(1)} %all_gather.3.screens), custom_call_target="tpu_custom_call" | custom-call | bytes 65536 | tf_op jit(solution)/shard_map/level_kernel/pallas_call | solution.py:333
  73.5 32.1 %conditional.2 = ((f32[2,3,256,256]{3,2,1,0:T(8,128)}, f32[2,2,256,256]{3,2,1,0:T(8,128)}, bf16[2,256,2048]{2,1,0:T(8,128)(2,1)}, bf16[2,256,2048]{2,1,0:T(8,128...) conditional(s32[]{:T(128)} %bitcast, () %tuple.37, ...), branch_computations={%region_0.0_spmd, %region_1.0_spmd} | conditional | flops 3221225472 | bytes 93323336 | solution.py:335
  73.5 0.4 collective-permute-start
  73.9 13.0 %collective-permute-done.other = bf16[2,256,2,4096]{3,2,1,0:T(2,128)(2,1)S(1)} collective-permute-done((bf16[2,256,2,4096]{3,2,1,0:T(2,128)(2,1)}, bf16[2,256,2,4096]{3,2,1,0:T(2,128)(2,1)S(1)}, u32[]{:S(2)}, u32[]{:S(2)}) %collective-permute-start) | collective-permute-done | bytes 8388640 | tf_op jit(solution)/shard_map/cond/branch_1_fun/ppermute | solution.py:311
  87.0 0.0 copy-start
  87.0 3.2 %copy-done = bf16[2,256,2,4096]{3,2,1,0:T(2,128)(2,1)} copy-done((bf16[2,256,2,4096]{3,2,1,0:T(2,128)(2,1)}, bf16[2,256,2,4096]{3,2,1,0:T(2,128)(2,1)S(1)}, u32[]{:S(2)}) %copy-start) | copy-done | bytes 8388632 | tf_op jit(solution)/shard_map/cond
  90.2 15.4 %inner_kernel.1 = (f32[2,3,256,256]{3,2,1,0:T(8,128)}, f32[2,2,256,256]{3,2,1,0:T(8,128)}, bf16[2,256,2048]{2,1,0:T(8,128)(2,1)}, bf16[2,256,2048]{2,1,0:T(8,128...) custom-call(s32[8,128]{1,0:T(8,128)S(1)} %get-tuple-element.49.own, ...), custom_call_target="tpu_custom_call" | custom-call | flops 3221225472 | bytes 26214400 | tf_op jit(solution)/shard_map/cond/branch_1_fun/inner_kernel/pallas_call | solution.py:312
  105.6 16.6 %conditional.3 = (f32[256,256]{1,0:T(8,128)S(1)}) conditional(s32[]{:T(128)} %bitcast.1, () %tuple.39, (bf16[8,2,256,128]{3,2,1,0:T(8,128)(2,1)}, s32[8,128]{1,0:T(8,128)S(1)}, s32[8,128]{1,0:T(8,128)S(1)}, bf16[8,2,256,128]{3,2,1,0:T(8,128)(2,1)S(1)}) %tuple.40, (bf16[8,2,256,128]{3,2,1,0:T(8,128)(2,1)}, ...), branch_computations={%region_2.0_spmd, %region_3.0_spmd, %region_4.0_spmd, %region_5.0_... | conditional | flops 536870912 | bytes 8388656 | solution.py:348
  105.6 1.0 slice.12
  106.7 4.5 %collective-permute-start.3 = (bf16[3,2,256,128]{3,2,1,0:T(8,128)(2,1)S(1)}, bf16[3,2,256,128]{3,2,1,0:T(8,128)(2,1)S(1)}, u32[]{:S(2)}, u32[]{:S(2)}) collective-permute-start(bf16[3,2,256,128]{3,2,1,0:T(8,128)(2,1)S(1)} %slice.12), channel_id=1, source_target_pairs={{1,2},{2,1},{3,4},{4,3},{5,6},{6,5},{7,8},{8,7},{9,10},{10,9},{11,... | collective-permute-start | bytes 1179656 | tf_op jit(solution)/shard_map/cond/branch_3_fun/ppermute | solution.py:341
  111.1 9.7 %collective-permute-done.3.got = bf16[3,2,256,128]{3,2,1,0:T(8,128)(2,1)S(1)} collective-permute-done((bf16[3,2,256,128]{3,2,1,0:T(8,128)(2,1)S(1)}, bf16[3,2,256,128]{3,2,1,0:T(8,128)(2,1)S(1)}, u32[]{:S(2)}, u32[]{:S(2)}) %collective-permute-start.3) | collective-permute-done | bytes 393248 | tf_op jit(solution)/shard_map/cond/branch_3_fun/ppermute | solution.py:341
  120.8 1.4 extra_kernel.8
  122.2 0.0 collective-permute-done.8.got
  122.2 3.6 %slow_kernel.1 = (f32[256,256]{1,0:T(8,128)S(1)}, f32[256,256]{1,0:T(8,128)S(1)}, f32[2,256,256]{2,1,0:T(8,128)S(1)}) custom-call(bf16[2,256,2048]{2,1,0:T(8,128)(2,1)S(1)} %collective-permute-done.8.got, bf16[2,256,2048]{2,1,0:T(8,128)(2,1)} %get-tuple-element.110.far, bf16[2,256,2048]{2,1,0:T(8,128)(2,1)} %get-tuple-element.111.near, ...), custom_call_target="tpu_custom_call" | custom-call | flops 1073741824 | bytes 8388608 | tf_op jit(solution)/shard_map/slow_kernel/pallas_call | solution.py:350
  125.9 3.6 %collective-permute-start.9 = (f32[2,256,256]{2,1,0:T(8,128)S(1)}, f32[2,256,256]{2,1,0:T(8,128)S(1)}, u32[]{:S(2)}, u32[]{:S(2)}) collective-permute-start(f32[2,256,256]{2,1,0:T(8,128)S(1)} %get-tuple-element.116), channel_id=1, source_target_pairs={{1,2},{2,1},{3,4},{4,3},{5,6},{6,5},{7,8},{8,7},{9,10},{10,9},{11,... | collective-permute-start | bytes 1572872 | tf_op jit(solution)/shard_map/ppermute | solution.py:360
  129.5 10.2 %collective-permute-done.9.back = f32[2,256,256]{2,1,0:T(8,128)S(1)} collective-permute-done((f32[2,256,256]{2,1,0:T(8,128)S(1)}, f32[2,256,256]{2,1,0:T(8,128)S(1)}, u32[]{:S(2)}, u32[]{:S(2)}) %collective-permute-start.9) | collective-permute-done | bytes 524320 | tf_op jit(solution)/shard_map/ppermute | solution.py:360
  139.7 1.6 %last_kernel.1 = (f32[2,3,256,256]{3,2,1,0:T(8,128)}, f32[2,2,256,256]{3,2,1,0:T(8,128)}) custom-call(s32[8,128]{1,0:T(8,128)S(1)} %get-tuple-element.106.own, s32[8,128]{1,0:T(8,128)S(1)} %collective-permute-done.7.below, f32[256,256]{1,0:T(8,128)S(1)} %get-tuple-element.114.far_near, ...), custom_call_target="tpu_custom_call", output_to_operand_aliasing={{0}: (5, {}), {1}: (6, {})} | custom-call | bytes 2097152 | tf_op jit(solution)/shard_map/last_kernel/pallas_call | solution.py:361
Async XLA Ops:
  2.0 13.0 %copy-start.1 = (s32[8,128]{1,0:T(8,128)S(1)}, s32[8,128]{1,0:T(8,128)}, u32[]{:S(2)}) copy-start(s32[8,128]{1,0:T(8,128)} %get-tuple-element.108) | copy-start | bytes 12292
  2.0 4.4 %collective-permute-start.7 = (s32[8,128]{1,0:T(8,128)S(1)}, s32[8,128]{1,0:T(8,128)S(1)}, u32[]{:S(2)}, u32[]{:S(2)}) collective-permute-start(s32[8,128]{1,0:T(8,128)S(1)} %get-tuple-element.106.own), channel_id=1, source_target_pairs={{0,1},{1,2},{2,3},{3,4},{4,5},{5,6},{6,7},{7,8},{8,9},{9,10},{10,1... | collective-permute-start | bytes 12296 | tf_op jit(solution)/shard_map/ppermute | solution.py:289
  10.8 111.4 %collective-permute-start.8 = (bf16[2,256,2048]{2,1,0:T(8,128)(2,1)}, bf16[2,256,2048]{2,1,0:T(8,128)(2,1)S(1)}, u32[]{:S(2)}, u32[]{:S(2)}) collective-permute-start(bf16[2,256,2048]{2,1,0:T(8,128)(2,1)} %pack_kernel.1), channel_id=1, source_target_pairs={{1,2},{2,1},{3,4},{4,3},{5,6},{6,5},{7,8},{8,7},{9,10},{10,9},{11,... | collective-permute-start | bytes 6291464 | tf_op jit(solution)/shard_map/ppermute | solution.py:303
  73.5 13.4 %collective-permute-start = (bf16[2,256,2,4096]{3,2,1,0:T(2,128)(2,1)}, bf16[2,256,2,4096]{3,2,1,0:T(2,128)(2,1)S(1)}, u32[]{:S(2)}, u32[]{:S(2)}) collective-permute-start(bf16[2,256,2,4096]{3,2,1,0:T(2,128)(2,1)} %get-tuple-element.59.bfac), channel_id=1, source_target_pairs={{0,1},{1,0},{2,3},{3,2},{4,5},{5,4},{6,7},{7,6},{8,9},{9,8},{10,11... | collective-permute-start | bytes 25165832 | tf_op jit(solution)/shard_map/cond/branch_1_fun/ppermute | solution.py:311
  87.0 3.2 %copy-start = (bf16[2,256,2,4096]{3,2,1,0:T(2,128)(2,1)}, bf16[2,256,2,4096]{3,2,1,0:T(2,128)(2,1)S(1)}, u32[]{:S(2)}) copy-start(bf16[2,256,2,4096]{3,2,1,0:T(2,128)(2,1)S(1)} %collective-permute-done.other) | copy-start | bytes 25165828 | tf_op jit(solution)/shard_map/cond
  106.7 14.1 %collective-permute-start.3 = (bf16[3,2,256,128]{3,2,1,0:T(8,128)(2,1)S(1)}, bf16[3,2,256,128]{3,2,1,0:T(8,128)(2,1)S(1)}, u32[]{:S(2)}, u32[]{:S(2)}) collective-permute-start(bf16[3,2,256,128]{3,2,1,0:T(8,128)(2,1)S(1)} %slice.12), channel_id=1, source_target_pairs={{1,2},{2,1},{3,4},{4,3},{5,6},{6,5},{7,8},{8,7},{9,10},{10,9},{11,... | collective-permute-start | bytes 1179656 | tf_op jit(solution)/shard_map/cond/branch_3_fun/ppermute | solution.py:341
  125.9 13.9 %collective-permute-start.9 = (f32[2,256,256]{2,1,0:T(8,128)S(1)}, f32[2,256,256]{2,1,0:T(8,128)S(1)}, u32[]{:S(2)}, u32[]{:S(2)}) collective-permute-start(f32[2,256,256]{2,1,0:T(8,128)S(1)} %get-tuple-element.116), channel_id=1, source_target_pairs={{1,2},{2,1},{3,4},{4,3},{5,6},{6,5},{7,8},{8,7},{9,10},{10,9},{11,... | collective-permute-start | bytes 1572872 | tf_op jit(solution)/shard_map/ppermute | solution.py:360

commit v2 on v1

--- a/solution.py
+++ b/solution.py
@@ -300,6 +300,7 @@
         6 * 2**20,
         vmem=60,
     )(own, below, bfac)
+    main, screens = lax.optimization_barrier((main, screens))
     main_got = lax.ppermute(main, "wide", slow)
 
     band = shape((2, 3, rows, rows), f32)

time: 143 us -> 119 us (0.83)
  blocking collectives: 55 us -> 18 us
  waiting for transfers between devices: 33.7 us -> 51.6 us
  starting transfers between devices: 16.4 us -> 11.6 us
    all_gather x1, blocking collectives: 55 us -> 18 us  [per_device(): screens = lax.all_gather(again, 'wide', tiled=True)]
    ppermute x1, waiting for transfers between devices: 9.66 us -> 30 us  [branch(): got = lax.ppermute(extra[:count], 'wide', slow)]
    ppermute x1, starting transfers between devices: 4.19 us -> 1.92 us  [per_device(): main_got = lax.ppermute(main, 'wide', slow)]
    ppermute x1, starting transfers between devices: 3.63 us -> 1.92 us  [per_device(): back_got = lax.ppermute(back, 'wide', slow)]
    ppermute x1, waiting for transfers between devices: 10.2 us -> 8.57 us  [per_device(): back_got = lax.ppermute(back, 'wide', slow)]
  transfers between devices with their start and end apart: 5 -> 5, of which waited for: 4 -> 3; matrix products, arithmetic and copies ran while one was open for 1% -> 1% of each run, Pallas kernels for 13% -> 16%
where the time goes in v2:
time: 119 us; the launch traced here: 117 us
  waiting for transfers between devices  51.6 us (43%)
  Pallas kernels  29.3 us (25%)
  blocking collectives  18 us (15%)
  starting transfers between devices  11.6 us (10%)
  local copies, waits for them, and re-layouts  4.41 us (4%)
  between operations  2.01 us (2%)
    ppermute x1, waiting for transfers between devices, branch(): got = lax.ppermute(extra[:count], 'wide', slow)  30 us
    all_gather x1, blocking collectives, per_device(): screens = lax.all_gather(again, 'wide', tiled=True)  18 us
    pallas_call x1, Pallas kernels, inner(): call(inner_kernel, n, inner_outs, [SMEM, SMEM, HBM, HBM], (HBM, HBM, VMEM...  15.4 us
    ppermute x1, waiting for transfers between devices, inner(): other = lax.ppermute(bfac, 'wide', fast)  13 us
    ppermute x1, waiting for transfers between devices, per_device(): back_got = lax.ppermute(back, 'wide', slow)  8.57 us
    pallas_call x1, Pallas kernels, per_device(): call(pack_kernel, n, window, [SMEM, SMEM, HBM], VMEM, [pltpu.VMEM((rows,...  4.36 us
    ppermute x1, starting transfers between devices, per_device(): below = lax.ppermute(own, 'wide', [(i, i + 1) for i in range(n - 1)])  3.68 us
    pallas_call x1, Pallas kernels, per_device(): call(slow_kernel, n, (square, square, shape((2, rows, rows), f32)), [VMEM...  3.63 us
  transfers between devices with their start and end apart: 5, of which 3 were waited for; matrix products, arithmetic and copies ran while one was open for 1% of the time, Pallas kernels for 16%

profile of v2, /device:TPU:9, one launch (start us, length us, event | category | flops | bytes accessed | tf_op | source)
XLA Modules:
  0.0 117.0 jit_solution(6048848471620502649)
XLA Ops:
  0.6 1.3 %screen_kernel.1 = (s32[8,128]{1,0:T(8,128)S(1)}, s32[8,128]{1,0:T(8,128)}) custom-call(s32[2,3]{1,0:T(2,128)} %pair_mask.1, s32[2,3]{1,0:T(2,128)} %dom_start.1), custom_call_target="tpu_custom_call" | custom-call | bytes 16384 | tf_op jit(solution)/shard_map/screen_kernel/pallas_call | solution.py:286
  2.0 3.7 %collective-permute-start.7 = (s32[8,128]{1,0:T(8,128)S(1)}, s32[8,128]{1,0:T(8,128)S(1)}, u32[]{:S(2)}, u32[]{:S(2)}) collective-permute-start(s32[8,128]{1,0:T(8,128)S(1)} %get-tuple-element.110.own), channel_id=1, source_target_pairs={{0,1},{1,2},{2,3},{3,4},{4,5},{5,6},{6,7},{7,8},{8,9},{9,10},{10,1... | collective-permute-start | bytes 12296 | tf_op jit(solution)/shard_map/ppermute | solution.py:289
  5.6 18.0 %all_gather.3.screens = s32[128,128]{1,0:T(8,128)S(1)} all-gather(s32[8,128]{1,0:T(8,128)} %get-tuple-element.108), channel_id=1, replica_groups=mesh['groups'=2,'wide'=16] {'wide'}, dimensions={0}, use_global_device_ids=true | all-gather | bytes 69632 | tf_op jit(solution)/shard_map/all_gather | solution.py:290
  23.6 0.0 collective-permute-done.7.below
  23.6 4.4 %pack_kernel.1 = bf16[2,256,2048]{2,1,0:T(8,128)(2,1)} custom-call(s32[8,128]{1,0:T(8,128)S(1)} %get-tuple-element.110.own, s32[8,128]{1,0:T(8,128)S(1)} %collective-permute-done.7.below, bf16[2,256,2,4096]{3,2,1,0:T(2,128)(2,1)} %bfac.1), custom_call_target="tpu_custom_call" | custom-call | bytes 6291456 | tf_op jit(solution)/shard_map/pack_kernel/pallas_call | solution.py:292
  28.0 1.9 %collective-permute-start.8 = (bf16[2,256,2048]{2,1,0:T(8,128)(2,1)}, bf16[2,256,2048]{2,1,0:T(8,128)(2,1)S(1)}, u32[]{:S(2)}, u32[]{:S(2)}) collective-permute-start(bf16[2,256,2048]{2,1,0:T(8,128)(2,1)} %pack_kernel.1), channel_id=1, source_target_pairs={{1,2},{2,1},{3,4},{4,3},{5,6},{6,5},{7,8},{8,7},{9,10},{10,9},{11,... | collective-permute-start | bytes 6291464 | tf_op jit(solution)/shard_map/ppermute | solution.py:304
  29.9 2.3 %level_kernel.1 = s32[1]{0:T(128)} custom-call(s32[128,128]{1,0:T(8,128)S(1)} %all_gather.3.screens), custom_call_target="tpu_custom_call" | custom-call | bytes 65536 | tf_op jit(solution)/shard_map/level_kernel/pallas_call | solution.py:334
  33.5 32.3 %conditional.2 = ((f32[2,3,256,256]{3,2,1,0:T(8,128)}, f32[2,2,256,256]{3,2,1,0:T(8,128)}, bf16[2,256,2048]{2,1,0:T(8,128)(2,1)}, bf16[2,256,2048]{2,1,0:T(8,128...) conditional(s32[]{:T(128)} %bitcast, () %tuple.39, ...), branch_computations={%region_0.0_spmd, %region_1.0_spmd} | conditional | flops 3221225472 | bytes 93323336 | solution.py:336
  33.5 0.7 collective-permute-start
  34.2 13.0 %collective-permute-done.other = bf16[2,256,2,4096]{3,2,1,0:T(2,128)(2,1)S(1)} collective-permute-done((bf16[2,256,2,4096]{3,2,1,0:T(2,128)(2,1)}, bf16[2,256,2,4096]{3,2,1,0:T(2,128)(2,1)S(1)}, u32[]{:S(2)}, u32[]{:S(2)}) %collective-permute-start) | collective-permute-done | bytes 8388640 | tf_op jit(solution)/shard_map/cond/branch_1_fun/ppermute | solution.py:312
  47.2 0.0 copy-start
  47.2 3.2 %copy-done = bf16[2,256,2,4096]{3,2,1,0:T(2,128)(2,1)} copy-done((bf16[2,256,2,4096]{3,2,1,0:T(2,128)(2,1)}, bf16[2,256,2,4096]{3,2,1,0:T(2,128)(2,1)S(1)}, u32[]{:S(2)}) %copy-start) | copy-done | bytes 8388632 | tf_op jit(solution)/shard_map/cond
  50.4 15.4 %inner_kernel.1 = (f32[2,3,256,256]{3,2,1,0:T(8,128)}, f32[2,2,256,256]{3,2,1,0:T(8,128)}, bf16[2,256,2048]{2,1,0:T(8,128)(2,1)}, bf16[2,256,2048]{2,1,0:T(8,128...) custom-call(s32[8,128]{1,0:T(8,128)S(1)} %get-tuple-element.49.own, ...), custom_call_target="tpu_custom_call" | custom-call | flops 3221225472 | bytes 26214400 | tf_op jit(solution)/shard_map/cond/branch_1_fun/inner_kernel/pallas_call | solution.py:313
  65.8 35.4 %conditional.3 = (f32[256,256]{1,0:T(8,128)S(1)}) conditional(s32[]{:T(128)} %bitcast.1, () %tuple.41, (bf16[8,2,256,128]{3,2,1,0:T(8,128)(2,1)}, s32[8,128]{1,0:T(8,128)S(1)}, s32[8,128]{1,0:T(8,128)S(1)}, bf16[8,2,256,128]{3,2,1,0:T(8,128)(2,1)S(1)}) %tuple.42, (bf16[8,2,256,128]{3,2,1,0:T(8,128)(2,1)}, ...), branch_computations={%region_2.0_spmd, %region_3.0_spmd, %region_4.0_spmd, %region_5.0_... | conditional | flops 536870912 | bytes 8388656 | solution.py:349
  65.9 1.2 %slice.14 = bf16[6,2,256,128]{3,2,1,0:T(8,128)(2,1)S(1)} slice(bf16[8,2,256,128]{3,2,1,0:T(8,128)(2,1)} %get-tuple-element.84), slice={[0:6], [0:2], [0:256], [0:128]} | slice | bytes 1572864 | tf_op jit(solution)/shard_map/cond/branch_5_fun/slice | solution.py:342
  67.1 3.4 %collective-permute-start.5 = (bf16[6,2,256,128]{3,2,1,0:T(8,128)(2,1)S(1)}, bf16[6,2,256,128]{3,2,1,0:T(8,128)(2,1)S(1)}, u32[]{:S(2)}, u32[]{:S(2)}) collective-permute-start(bf16[6,2,256,128]{3,2,1,0:T(8,128)(2,1)S(1)} %slice.14), channel_id=1, source_target_pairs={{1,2},{2,1},{3,4},{4,3},{5,6},{6,5},{7,8},{8,7},{9,10},{10,9},{11,... | collective-permute-start | bytes 2359304 | tf_op jit(solution)/shard_map/cond/branch_5_fun/ppermute | solution.py:342
  70.5 30.0 %collective-permute-done.5.got = bf16[6,2,256,128]{3,2,1,0:T(8,128)(2,1)S(1)} collective-permute-done((bf16[6,2,256,128]{3,2,1,0:T(8,128)(2,1)S(1)}, bf16[6,2,256,128]{3,2,1,0:T(8,128)(2,1)S(1)}, u32[]{:S(2)}, u32[]{:S(2)}) %collective-permute-start.5) | collective-permute-done | bytes 786464 | tf_op jit(solution)/shard_map/cond/branch_5_fun/ppermute | solution.py:342
  100.5 0.7 extra_kernel.10
  101.2 0.0 collective-permute-done.8.got
  101.2 3.6 %slow_kernel.1 = (f32[256,256]{1,0:T(8,128)S(1)}, f32[256,256]{1,0:T(8,128)S(1)}, f32[2,256,256]{2,1,0:T(8,128)S(1)}) custom-call(bf16[2,256,2048]{2,1,0:T(8,128)(2,1)S(1)} %collective-permute-done.8.got, bf16[2,256,2048]{2,1,0:T(8,128)(2,1)} %get-tuple-element.114.far, bf16[2,256,2048]{2,1,0:T(8,128)(2,1)} %get-tuple-element.115.near, ...), custom_call_target="tpu_custom_call" | custom-call | flops 1073741824 | bytes 8388608 | tf_op jit(solution)/shard_map/slow_kernel/pallas_call | solution.py:351
  104.8 1.9 %collective-permute-start.9 = (f32[2,256,256]{2,1,0:T(8,128)S(1)}, f32[2,256,256]{2,1,0:T(8,128)S(1)}, u32[]{:S(2)}, u32[]{:S(2)}) collective-permute-start(f32[2,256,256]{2,1,0:T(8,128)S(1)} %get-tuple-element.120), channel_id=1, source_target_pairs={{1,2},{2,1},{3,4},{4,3},{5,6},{6,5},{7,8},{8,7},{9,10},{10,9},{11,... | collective-permute-start | bytes 1572872 | tf_op jit(solution)/shard_map/ppermute | solution.py:361
  106.8 8.6 %collective-permute-done.9.back = f32[2,256,256]{2,1,0:T(8,128)S(1)} collective-permute-done((f32[2,256,256]{2,1,0:T(8,128)S(1)}, f32[2,256,256]{2,1,0:T(8,128)S(1)}, u32[]{:S(2)}, u32[]{:S(2)}) %collective-permute-start.9) | collective-permute-done | bytes 524320 | tf_op jit(solution)/shard_map/ppermute | solution.py:361
  115.3 1.6 %last_kernel.1 = (f32[2,3,256,256]{3,2,1,0:T(8,128)}, f32[2,2,256,256]{3,2,1,0:T(8,128)}) custom-call(s32[8,128]{1,0:T(8,128)S(1)} %get-tuple-element.110.own, s32[8,128]{1,0:T(8,128)S(1)} %collective-permute-done.7.below, f32[256,256]{1,0:T(8,128)S(1)} %get-tuple-element.118.far_near, ...), custom_call_target="tpu_custom_call", output_to_operand_aliasing={{0}: (5, {}), {1}: (6, {})} | custom-call | bytes 2097152 | tf_op jit(solution)/shard_map/last_kernel/pallas_call | solution.py:362
Async XLA Ops:
  2.0 21.7 %collective-permute-start.7 = (s32[8,128]{1,0:T(8,128)S(1)}, s32[8,128]{1,0:T(8,128)S(1)}, u32[]{:S(2)}, u32[]{:S(2)}) collective-permute-start(s32[8,128]{1,0:T(8,128)S(1)} %get-tuple-element.110.own), channel_id=1, source_target_pairs={{0,1},{1,2},{2,3},{3,4},{4,5},{5,6},{6,7},{7,8},{8,9},{9,10},{10,1... | collective-permute-start | bytes 12296 | tf_op jit(solution)/shard_map/ppermute | solution.py:289
  28.0 73.2 %collective-permute-start.8 = (bf16[2,256,2048]{2,1,0:T(8,128)(2,1)}, bf16[2,256,2048]{2,1,0:T(8,128)(2,1)S(1)}, u32[]{:S(2)}, u32[]{:S(2)}) collective-permute-start(bf16[2,256,2048]{2,1,0:T(8,128)(2,1)} %pack_kernel.1), channel_id=1, source_target_pairs={{1,2},{2,1},{3,4},{4,3},{5,6},{6,5},{7,8},{8,7},{9,10},{10,9},{11,... | collective-permute-start | bytes 6291464 | tf_op jit(solution)/shard_map/ppermute | solution.py:304
  33.5 13.7 %collective-permute-start = (bf16[2,256,2,4096]{3,2,1,0:T(2,128)(2,1)}, bf16[2,256,2,4096]{3,2,1,0:T(2,128)(2,1)S(1)}, u32[]{:S(2)}, u32[]{:S(2)}) collective-permute-start(bf16[2,256,2,4096]{3,2,1,0:T(2,128)(2,1)} %get-tuple-element.59.bfac), channel_id=1, source_target_pairs={{0,1},{1,0},{2,3},{3,2},{4,5},{5,4},{6,7},{7,6},{8,9},{9,8},{10,11... | collective-permute-start | bytes 25165832 | tf_op jit(solution)/shard_map/cond/branch_1_fun/ppermute | solution.py:312
  47.2 3.2 %copy-start = (bf16[2,256,2,4096]{3,2,1,0:T(2,128)(2,1)}, bf16[2,256,2,4096]{3,2,1,0:T(2,128)(2,1)S(1)}, u32[]{:S(2)}) copy-start(bf16[2,256,2,4096]{3,2,1,0:T(2,128)(2,1)S(1)} %collective-permute-done.other) | copy-start | bytes 25165828 | tf_op jit(solution)/shard_map/cond
  67.1 33.4 %collective-permute-start.5 = (bf16[6,2,256,128]{3,2,1,0:T(8,128)(2,1)S(1)}, bf16[6,2,256,128]{3,2,1,0:T(8,128)(2,1)S(1)}, u32[]{:S(2)}, u32[]{:S(2)}) collective-permute-start(bf16[6,2,256,128]{3,2,1,0:T(8,128)(2,1)S(1)} %slice.14), channel_id=1, source_target_pairs={{1,2},{2,1},{3,4},{4,3},{5,6},{6,5},{7,8},{8,7},{9,10},{10,9},{11,... | collective-permute-start | bytes 2359304 | tf_op jit(solution)/shard_map/cond/branch_5_fun/ppermute | solution.py:342
  104.8 10.5 %collective-permute-start.9 = (f32[2,256,256]{2,1,0:T(8,128)S(1)}, f32[2,256,256]{2,1,0:T(8,128)S(1)}, u32[]{:S(2)}, u32[]{:S(2)}) collective-permute-start(f32[2,256,256]{2,1,0:T(8,128)S(1)} %get-tuple-element.120), channel_id=1, source_target_pairs={{1,2},{2,1},{3,4},{4,3},{5,6},{6,5},{7,8},{8,7},{9,10},{10,9},{11,... | collective-permute-start | bytes 1572872 | tf_op jit(solution)/shard_map/ppermute | solution.py:361
